TPU v7x, 32 devices: a whole 2x2x4 slice. The times are simulated.
32 devices in a mesh: win: 16 (over z, y, core), chan: 2 (over x).
Axes of the slice: x: 2, y: 2, z: 4, core: 2. Of those that a mesh axis runs over, the one named last changes fastest.
Arguments:
- traces: bfloat16 [32, 512, 4096], P('win', 'chan'), may hold values from -120 to 120
- block_pairs: int32 [16, 2], replicated, may hold values from 0 to 3
- valid_count: int32 [1], replicated, may hold values from 4 to 15
Outputs:
- cross_spectra: float32 [16, 8, 2, 128, 128], P('win', 'chan')
Inputs may be any that keep to these rules, and one draw needn't show every extreme that they name: `block_pairs`: entries are channel block numbers; a pair may repeat.
All inputs are finite; a program needn't handle non-finite values.
Results may differ from a plain program's by a relative error of at most 0.0037.
Values may be sent and summed in bfloat16 or wider, within the bound.
A program may use at most 64 MiB of HBM per device.

v0:
```python
import math

import jax
import jax.numpy as jnp
from jax import lax
from jax.sharding import PartitionSpec as P

BLOCK = 128
NBINS = 256
FREQ_LO = 64
GROUP = 32


EPS = 1e-06


def dft_table(length, first_bin, bins):
    times = jnp.arange(length, dtype=jnp.int32)
    freqs = first_bin + jnp.arange(bins, dtype=jnp.int32)
    phases = times[:, None] * freqs[None, :] % length
    angles = phases.astype(jnp.float32) * (2.0 * math.pi / length)
    factor = 1.0 / math.sqrt(length)
    return (jnp.concatenate([jnp.cos(angles), -jnp.sin(angles)], axis=1) * factor).astype(
        jnp.bfloat16
    )


def block_layout(band_part, block, group):
    windows, channels, _, width = band_part.shape
    shaped = band_part.reshape(windows, channels // block, block, 2, width // group, group)
    rotated = jnp.stack([shaped[:, :, :, 1], -shaped[:, :, :, 0]], axis=3)

    def arrange(values):
        moved = jnp.transpose(values, (1, 4, 2, 0, 3, 5))
        return moved.reshape(channels // block, width // group, block, windows * 2 * group)

    return (arrange(shaped), arrange(rotated))


def pair_products(upper_direct, upper_rotated, lower):
    upper = jnp.concatenate([upper_direct, upper_rotated], axis=2)
    products = jnp.einsum("pgik,pgjk->pgij", upper, lower, preferred_element_type=jnp.float32)
    return products.reshape(products.shape[0], products.shape[1], 2, lower.shape[2], lower.shape[2])


def pair_terms(direct, rotated, chosen):
    return pair_products(direct[chosen[:, 0]], rotated[chosen[:, 0]], direct[chosen[:, 1]])


def on_device(traces, block_pairs, valid_count):
    windows, channels, length = traces.shape
    spectra = jnp.dot(
        traces.reshape(windows * channels, length),
        dft_table(length, FREQ_LO, NBINS),
        preferred_element_type=jnp.float32,
    )
    energy = jnp.sum(spectra * spectra, axis=1, keepdims=True) / NBINS
    whitened = (
        (spectra * lax.rsqrt(energy + EPS))
        .astype(jnp.bfloat16)
        .reshape(windows, channels, 2, NBINS)
    )
    banded = lax.all_to_all(whitened, "chan", split_axis=3, concat_axis=1, tiled=True)
    stack_scale = 1.0 / math.sqrt(windows * lax.axis_size("win") * GROUP)
    slots = block_pairs.shape[0] // lax.axis_size("win")
    first_slot = lax.axis_index("win") * slots
    mine = lax.dynamic_slice_in_dim(block_pairs, first_slot, slots, 0)
    direct, rotated = block_layout(lax.all_gather(banded, "win", axis=0, tiled=True), BLOCK, GROUP)
    stacked = pair_terms(direct, rotated, mine)
    slot_ids = first_slot + jnp.arange(slots, dtype=jnp.int32)
    live = (slot_ids < valid_count[0]).astype(jnp.float32)
    return stacked * stack_scale * live[:, None, None, None, None]


def solution(mesh):
    in_specs = (P("win", "chan", None), P(), P())
    out_specs = P("win", "chan", None, None, None)
    return jax.shard_map(
        on_device, mesh=mesh, in_specs=in_specs, out_specs=out_specs, check_vma=False
    )
```

profile of v0, /device:TPU:8, one launch (start us, length us, event | category | flops | bytes accessed | tf_op | source)
XLA Modules:
  0.0 193.3 jit_solution(7894221395196936665)
XLA Ops:
  6.5 0.0 copy-start
  6.5 0.0 all-gather.2.cloned.1.call-start
  6.5 0.0 copy-start.2
  6.5 16.7 %fusion.15 = (f32[4096,256]{1,0:T(8,128)S(1)}, f32[4096,256]{1,0:T(8,128)S(1)}) fusion(s32[256]{0:T(256)S(1)} %iota_add_fusion), kind=kLoop, calls=%fused_computation.22 | loop fusion | flops 15728640 | bytes 8389632 | tf_op jit(solution)/shard_map/cos | solution.py:23
  23.3 0.0 copy-done.2
  23.3 2.5 %multiply_reduce_fusion = (f32[512]{0:T(512)S(1)}, f32[512,512]{1,0:T(8,128)S(1)}) fusion(bf16[512,4096]{1,0:T(8,128)(2,1)S(1)} %bitcast.43, f32[4096,256]{1,0:T(8,128)S(1)} %get-tuple-element.43, f32[4096,256]{1,0:T(8,128)S(1)} %get-tuple-element.42), kind=kOutput, calls=%fused_computation.24 | convolution fusion | flops 2154298880 | bytes 13633536 | tf_op jit(solution)/shard_map/dot_general | solution.py:52
  25.8 0.1 fusion.19
  25.9 0.1 reshape.57
  26.0 0.8 copy.18
  26.8 10.7 %all_to_all.18 = bf16[2,256,2,256]{1,2,0,3:T(2,128)(2,1)S(1)} all-to-all(bf16[2,256,2,256]{1,2,0,3:T(2,128)(2,1)S(1)} %copy.18), channel_id=1, replica_groups=mesh['win'=16,'chan'=2] {'chan'}, dimensions={3} | all-to-all | bytes 1048576 | tf_op jit(solution)/shard_map/all_to_all | solution.py:63
  37.5 0.1 copy.19
  37.6 1.0 copy.20
  38.6 0.0 all-gather.2.cloned.1.call-update
  38.6 0.0 copy-done
  38.6 0.1 constant_dynamic-slice_fusion.2
  38.7 0.6 fusion.25
  43.4 69.9 %all-gather.2.cloned.1.call-done = bf16[32,512,2,128]{3,1,2,0:T(8,128)(2,1)} async-done(((bf16[2,512,2,128]{3,1,2,0:T(8,128)(2,1)}), bf16[32,512,2,128]{3,1,2,0:T(8,128)(2,1)}) %all-gather.2.cloned.1.call-update) | async-done | bytes 8388624 | tf_op jit(solution)/shard_map/all_gather | solution.py:68
  113.3 12.0 %copy.21 = bf16[32,512,2,128]{1,3,2,0:T(8,128)(2,1)} copy(bf16[32,512,2,128]{3,1,2,0:T(8,128)(2,1)} %all-gather.2.cloned.1.call-done) | data formatting | bytes 16777216 | tf_op jit(solution)/shard_map/all_gather | solution.py:68
  125.3 12.5 %reshape.58 = bf16[32,4,128,2,4,32]{2,1,5,4,3,0:T(4,128)(2,1)} reshape(bf16[32,512,2,128]{1,3,2,0:T(8,128)(2,1)} %copy.21) | data formatting | bytes 16777216 | tf_op jit(solution)/shard_map/reshape | solution.py:30
  137.8 7.3 %fusion.24 = (bf16[32,4,128,1,4,32]{2,1,5,4,3,0:T(4,128)(2,1)S(1)}, bf16[32,4,128,1,4,32]{2,1,5,4,3,0:T(4,128)(2,1)}) fusion(bf16[32,4,128,2,4,32]{2,1,5,4,3,0:T(4,128)(2,1)} %reshape.58), kind=kLoop, calls=%fused_computation.36 | loop fusion | flops 2097152 | bytes 16777216 | tf_op jit(solution)/shard_map/slice | solution.py:31
  145.1 8.9 %copy.22 = bf16[4,4,128,32,2,32]{2,5,4,3,1,0:T(8,128)(2,1)} copy(bf16[4,4,128,32,2,32]{2,0,5,1,4,3:T(4,128)(2,1)} %bitcast.37) | data formatting | bytes 16777216 | tf_op jit(solution)/shard_map/transpose | solution.py:34
  154.0 8.2 %maximum_bitcast_fusion = bf16[4,4,128,32,2,32]{2,0,5,1,4,3:T(4,128)(2,1)} fusion(bf16[32,4,128,1,4,32]{2,1,5,4,3,0:T(4,128)(2,1)} %get-tuple-element.39, bf16[32,4,128,1,4,32]{2,1,5,4,3,0:T(4,128)(2,1)S(1)} %get-tuple-element.38), kind=kLoop, calls=%fused_computation.2 | loop fusion | flops 4194304 | bytes 16777216 | tf_op jit(solution)/shard_map/transpose | solution.py:34
  162.1 8.9 %copy.24 = bf16[4,4,128,32,2,32]{2,5,4,3,1,0:T(8,128)(2,1)} copy(bf16[4,4,128,32,2,32]{2,0,5,1,4,3:T(4,128)(2,1)} %maximum_bitcast_fusion) | data formatting | bytes 16777216 | tf_op jit(solution)/shard_map/transpose | solution.py:34
  171.0 3.9 %constant_dynamic-slice_fusion = (bf16[1,4,128,2048]{2,3,1,0:T(8,128)(2,1)}, bf16[1,4,128,2048]{2,3,1,0:T(8,128)(2,1)S(1)}) fusion(bf16[4,4,128,2048]{2,3,1,0:T(8,128)(2,1)} %bitcast.40, s32[]{:T(128)} %bitcast.8, bf16[4,4,128,2048]{2,3,1,0:T(8,128)(2,1)} %bitcast.38), kind=kLoop, calls=%fused_computation.29 | loop fusion | bytes 8388612 | tf_op jit(solution)/shard_map/gather | solution.py:47
  174.9 4.0 %copy.28 = bf16[1,4,128,2048]{3,2,1,0:T(8,128)(2,1)} copy(bf16[1,4,128,2048]{2,3,1,0:T(8,128)(2,1)} %get-tuple-element.46) | data formatting | bytes 4194304
  178.9 2.7 %copy.27 = bf16[1,4,128,2048]{3,2,1,0:T(8,128)(2,1)} copy(bf16[1,4,128,2048]{2,3,1,0:T(8,128)(2,1)S(1)} %get-tuple-element.47) | data formatting | bytes 4194304
  181.6 0.0 copy-start.1
  181.6 4.9 %fusion.16 = f32[4,256,128]{2,1,0:T(8,128)} fusion(bf16[4,4,128,2048]{2,3,1,0:T(8,128)(2,1)} %bitcast.39, s32[]{:T(128)} %bitcast.13, bf16[1,4,128,2048]{3,2,1,0:T(8,128)(2,1)} %copy.28, bf16[1,4,128,2048]{3,2,1,0:T(8,128)(2,1)} %copy.27, f32[]{:T(128)} %bitcast.16), kind=kOutput, calls=%fused_computation.25 | convolution fusion | flops 545390592 | bytes 6816768 | tf_op jit(solution)/shard_map/pgik,pgjk->pgij/dot_general | solution.py:42
  186.5 0.0 copy-done.1
  (2 shorter events, 0.0 us)
Async XLA Ops:
  6.5 32.1 %copy-start = (s32[16,2]{0,1:T(2,128)S(1)}, s32[16,2]{0,1:T(2,128)}, u32[]{:S(2)}) copy-start(s32[16,2]{0,1:T(2,128)} %param.4) | copy-start | bytes 388
  6.5 106.8 %all-gather.2.cloned.1.call-start = ((), (), s32[]{:S(2)}) async-start(), calls=%async_computation.1 | async-start | bytes 8912896 | tf_op jit(solution)/shard_map/all_gather | solution.py:68
  6.5 16.7 %copy-start.2 = (bf16[2,256,4096]{2,1,0:T(8,128)(2,1)S(1)}, bf16[2,256,4096]{2,1,0:T(8,128)(2,1)}, u32[]{:S(2)}) copy-start(bf16[2,256,4096]{2,1,0:T(8,128)(2,1)} %param.3) | copy-start | bytes 12582916
  181.6 4.9 %copy-start.1 = (s32[16,2]{0,1:T(2,128)S(1)}, s32[16,2]{0,1:T(2,128)}, u32[]{:S(2)}) copy-start(s32[16,2]{0,1:T(2,128)} %param.4) | copy-start | bytes 388
Sparse Core Ops, SparseCore 0:
  38.7 74.5 all-gather.1
where the time goes:
time: 196 us; the launch traced here: 193 us
  waiting for transfers between devices  69.9 us (36%)
  local copies, waits for them, and re-layouts  55.5 us (28%)
  other arithmetic  32.3 us (16%)
  between operations  17.7 us (9%)
  blocking collectives  10.7 us (5%)
  matrix products  7.38 us (4%)
    all_gather x1, waiting for transfers between devices, on_device(): lax.all_gather(banded, 'win', axis=0, tiled=True)  69.9 us
    transpose x2, local copies, waits for them, and re-layouts, arrange(): moved = jnp.transpose(values, (1, 4, 2, 0, 3, 5))  17.8 us
    cos x1, other arithmetic, dft_table(): jnp.cos(angles)  16.7 us
    reshape x1, local copies, waits for them, and re-layouts, block_layout(): band_part.reshape(windows, channels // block, block, 2, width // group, g...  12.5 us
    all_gather x1, local copies, waits for them, and re-layouts, on_device(): lax.all_gather(banded, 'win', axis=0, tiled=True)  12 us
    all_to_all x1, blocking collectives, on_device(): lax.all_to_all(whitened, 'chan', split_axis=3, concat_axis=1, tiled=True)  10.7 us
    transpose x1, other arithmetic, arrange(): moved = jnp.transpose(values, (1, 4, 2, 0, 3, 5))  8.19 us
    slice x1, other arithmetic, block_layout(): rotated = jnp.stack([shaped[:, :, :, 1], -shaped[:, :, :, 0]], axis=3)  7.26 us
  transfers between devices with their start and end apart: 1, of which 1 were waited for; matrix products, arithmetic and copies ran while one was open for 0% of the time, Pallas kernels for 0%

commit v1 on v0

v1 whole, which is shorter than its diff:
```python
import functools
import math

import jax
import jax.numpy as jnp
import ml_dtypes
import numpy as np
from jax import lax
from jax.experimental import pallas as pl
from jax.experimental.pallas import tpu as pltpu
from jax.sharding import PartitionSpec as P

BLOCK = 128
NBINS = 256
FREQ_LO = 64
GROUP = 32
GROUPS = NBINS // GROUP
EPS = 1e-06
MESH = pl.DeviceIdType.MESH
KCH = 4


def dft_table(length):
    times = np.arange(length, dtype=np.int32)
    freqs = FREQ_LO + np.arange(NBINS, dtype=np.int32)
    phases = times[:, None] * freqs[None, :] % length
    angles = phases.astype(np.float32) * np.float32(2.0 * math.pi / length)
    wide = angles.astype(np.float64)
    factor = np.float32(1.0 / math.sqrt(length))
    re = np.cos(wide).astype(np.float32) * factor
    im = -np.sin(wide).astype(np.float32) * factor
    table = np.stack(
        [re.reshape(length, GROUPS, GROUP), im.reshape(length, GROUPS, GROUP)], axis=2
    )
    return table.reshape(length, 2 * NBINS).astype(ml_dtypes.bfloat16)


def kernel(
    dims, tr_hbm, table_hbm, pairs, out,
    tr, table, acc, send, held, turned, outbox, inbox, relay, mail, done,
    in_sem, self_sem, a_send, a_recv, p_send, p_recv, r_recv, f_send, f_recv,
):
    planes, sub, chans, spp, spd, chl, length, relayed = dims
    win, x = lax.axis_index("win"), lax.axis_index("chan")
    q, j = win // sub, win % sub
    g = x * sub + j
    kc = length // KCH
    nch = chl // BLOCK

    def tr_copy(c, k):
        part = (slice(None), pl.ds(c * BLOCK, BLOCK), pl.ds(k * kc, kc))
        return pltpu.make_async_copy(tr_hbm.at[part], tr.at[part], in_sem.at[c * KCH + k])

    def table_copy(k):
        part = pl.ds(k * kc, kc)
        return pltpu.make_async_copy(table_hbm.at[part], table.at[part], in_sem.at[nch * KCH + k])

    for k in range(KCH):
        tr_copy(0, k).start()
        table_copy(k).start()
    for c in range(1, nch):
        for k in range(KCH):
            tr_copy(c, k).start()

    barrier = pltpu.get_barrier_semaphore()

    @pl.loop(1, GROUPS)
    def _(o):
        to = (g + o) % GROUPS
        pl.semaphore_signal(
            barrier, inc=1, device_id=(q * sub + to % sub, to // sub), device_id_type=MESH
        )

    @pl.loop(1, planes)
    def _(o):
        pl.semaphore_signal(
            barrier, inc=1, device_id=(((q + o) % planes) * sub + j, x), device_id_type=MESH
        )

    def a_copy(c, o, to):
        return pltpu.make_async_remote_copy(
            src_ref=send.at[to, pl.ds(c * BLOCK, BLOCK), :],
            dst_ref=held.at[j, x * nch + c],
            send_sem=a_send.at[c, o],
            recv_sem=a_recv.at[c, o],
            device_id=(q * sub + to % sub, to // sub),
            device_id_type=MESH,
        )

    low = lax.broadcasted_iota(jnp.int32, (BLOCK, 128), 1) < 2 * GROUP
    for c in range(nch):
        for k in range(KCH):
            tr_copy(c, k).wait()
            if c == 0:
                table_copy(k).wait()
            rows = tr[:, c * BLOCK : (c + 1) * BLOCK, k * kc : (k + 1) * kc]
            term = jnp.dot(
                rows.reshape(2 * BLOCK, kc),
                table[k * kc : (k + 1) * kc, :],
                preferred_element_type=jnp.float32,
            )
            if k == 0:
                acc[...] = term
            else:
                acc[...] += term
        spectra = acc[...]
        energy = jnp.sum(spectra * spectra, axis=1, keepdims=True) / NBINS
        white = spectra * lax.rsqrt(energy + EPS)
        for h in range(GROUPS // 2):
            a = white[:BLOCK, h * 128 : (h + 1) * 128]
            b = white[BLOCK:, h * 128 : (h + 1) * 128]
            even = jnp.where(low, a, pltpu.roll(b, 64, 1))
            odd = jnp.where(low, pltpu.roll(a, 64, 1), b)
            send[2 * h, c * BLOCK : (c + 1) * BLOCK, :] = even.astype(jnp.bfloat16)
            send[2 * h + 1, c * BLOCK : (c + 1) * BLOCK, :] = odd.astype(jnp.bfloat16)
        if c == 0:
            pl.semaphore_wait(barrier, GROUPS - 1 + planes - 1)

        @pl.loop(1, GROUPS)
        def _(o):
            a_copy(c, o, (g + o) % GROUPS).start()

        pltpu.make_async_copy(
            send.at[g, pl.ds(c * BLOCK, BLOCK), :],
            held.at[j, x * nch + c],
            self_sem.at[c],
        ).start()

    for c in range(nch):
        pltpu.make_async_copy(
            send.at[g, pl.ds(c * BLOCK, BLOCK), :],
            held.at[j, x * nch + c],
            self_sem.at[c],
        ).wait()

        @pl.loop(1, GROUPS)
        def _(o):
            src = (g + GROUPS - o) % GROUPS
            pltpu.make_async_remote_copy(
                src_ref=send.at[src, pl.ds(c * BLOCK, BLOCK), :],
                dst_ref=held.at[src % sub, (src // sub) * nch + c],
                send_sem=a_send.at[c, o],
                recv_sem=a_recv.at[c, o],
                device_id=(q * sub + src % sub, src // sub),
                device_id_type=MESH,
            ).wait_recv()

    row = lax.broadcasted_iota(jnp.int32, (128, 128), 0)
    col = lax.broadcasted_iota(jnp.int32, (128, 128), 1)
    is_re = col % (2 * GROUP) < GROUP
    turn = jnp.where(
        is_re,
        jnp.where(row == col + GROUP, 1.0, 0.0),
        jnp.where(row + GROUP == col, -1.0, 0.0),
    ).astype(jnp.bfloat16)
    for m in range(sub):

        @pl.loop(0, chans * nch)
        def _(b):
            turned[m, b] = jnp.dot(
                held[m, b], turn, preferred_element_type=jnp.float32
            ).astype(jnp.bfloat16)

    def partial(p):
        r, s = pairs[p, 0], pairs[p, 1]
        upper = jnp.concatenate(
            [
                jnp.concatenate([held[m, r] for m in range(sub)], axis=1),
                jnp.concatenate([turned[m, r] for m in range(sub)], axis=1),
            ],
            axis=0,
        )
        lower = jnp.concatenate([held[m, s] for m in range(sub)], axis=1)
        return lax.dot_general(
            upper, lower, (((1,), (1,)), ((), ())), preferred_element_type=jnp.float32
        )

    first_half = q < planes // 2
    last = planes - 1

    def dest(k):
        return jnp.where(first_half, (q + planes - k) % planes, (q + k) % planes)

    def p_copy(d, i, to):
        return pltpu.make_async_remote_copy(
            src_ref=outbox.at[d, i],
            dst_ref=inbox.at[q, i],
            send_sem=p_send.at[d, i],
            recv_sem=p_recv.at[q, i],
            device_id=(to * sub + j, x),
            device_id_type=MESH,
        )

    def r_copy(d, i, to):
        return pltpu.make_async_remote_copy(
            src_ref=outbox.at[d, i],
            dst_ref=relay.at[i],
            send_sem=p_send.at[d, i],
            recv_sem=r_recv.at[i],
            device_id=(to * sub + j, x),
            device_id_type=MESH,
        )

    far = last - q
    far_relayed = jnp.logical_or(q == 0, q == last)
    relays = jnp.logical_or(q == 1, q == last - 1)
    rdest = jnp.where(q == 1, last, 0)
    rnext = jnp.where(q == 0, 1, last - 1)

    @pl.loop(0, (planes - 1) * spp)
    def _(n):
        d, i = dest(n // spp + 1), n % spp
        t = (j * spd + spd + i) % spp

        def send_out():
            outbox[d, i] = partial(d * spp + t).astype(jnp.bfloat16)

        if not relayed:
            send_out()
            p_copy(d, i, d).start()
        else:
            held_back = jnp.logical_and(relays, d == rdest)

            @pl.when(jnp.logical_not(held_back))
            def _():
                send_out()
                via = jnp.logical_and(far_relayed, d == far)

                @pl.when(via)
                def _():
                    r_copy(d, i, rnext).start()

                @pl.when(jnp.logical_not(via))
                def _():
                    p_copy(d, i, d).start()

    if relayed:

        @pl.when(relays)
        def _():
            @pl.loop(0, spp)
            def _(i):
                t = (j * spd + spd + i) % spp
                value = partial(rdest * spp + t)
                r_copy(rdest, i, rdest).wait_recv()
                outbox[rdest, i] = (value + relay[i].astype(jnp.float32)).astype(jnp.bfloat16)
                p_copy(rdest, i, rdest).start()

    def f_copy(t, owner):
        return pltpu.make_async_remote_copy(
            src_ref=done.at[t],
            dst_ref=mail.at[j, t % spd],
            send_sem=f_send.at[t],
            recv_sem=f_recv.at[j, t % spd],
            device_id=(q * sub + owner, x),
            device_id_type=MESH,
        )

    def through_relay(src):
        return jnp.logical_or(
            jnp.logical_and(q == last, src == 0), jnp.logical_and(q == 0, src == last)
        )

    @pl.loop(0, spp)
    def _(i):
        t = (j * spd + spd + i) % spp
        done[t] = partial(q * spp + t)

    @pl.loop(0, spp)
    def _(i):
        t = (j * spd + spd + i) % spp

        @pl.loop(1, planes)
        def _(o):
            src = (q + o) % planes

            def take():
                pltpu.make_async_remote_copy(
                    src_ref=outbox.at[src, i],
                    dst_ref=inbox.at[src, i],
                    send_sem=p_send.at[src, i],
                    recv_sem=p_recv.at[src, i],
                    device_id=(src * sub + j, x),
                    device_id_type=MESH,
                ).wait_recv()
                done[t] += inbox[src, i].astype(jnp.float32)

            if relayed:
                pl.when(jnp.logical_not(through_relay(src)))(take)
            else:
                take()

        @pl.when(t // spd != j)
        def _():
            f_copy(t, t // spd).start()

        @pl.when(t // spd == j)
        def _():
            out[t % spd, j] = done[t]

    for m in range(1, sub):
        src = (j + m) % sub
        for e in range(spd):
            pltpu.make_async_remote_copy(
                src_ref=done.at[e],
                dst_ref=mail.at[src, e],
                send_sem=f_send.at[e],
                recv_sem=f_recv.at[src, e],
                device_id=(q * sub + src, x),
                device_id_type=MESH,
            ).wait_recv()
            out[e, src] = mail[src, e]

    for c in range(nch):

        @pl.loop(1, GROUPS)
        def _(o):
            a_copy(c, o, (g + o) % GROUPS).wait_send()

    @pl.loop(0, (planes - 1) * spp)
    def _(n):
        d, i = dest(n // spp + 1), n % spp
        p_copy(d, i, d).wait_send()

    @pl.loop(0, spp)
    def _(t):
        @pl.when(t // spd != j)
        def _():
            f_copy(t, t // spd).wait_send()


def on_device(planes, sub, chans, table, traces, block_pairs, valid_count):
    windows, chl, length = traces.shape
    slots = block_pairs.shape[0]
    spp, spd = slots // planes, slots // (planes * sub)
    relayed = planes >= 4
    dims = (planes, sub, chans, spp, spd, chl, length, relayed)
    bf, f32 = jnp.bfloat16, jnp.float32
    nch = chl // BLOCK
    sums = pl.pallas_call(
        functools.partial(kernel, dims),
        name="cross_spectra",
        out_shape=jax.ShapeDtypeStruct((spd, sub, 2 * BLOCK, BLOCK), f32),
        in_specs=[
            pl.BlockSpec(memory_space=pl.ANY),
            pl.BlockSpec(memory_space=pl.ANY),
            pl.BlockSpec(memory_space=pltpu.SMEM),
        ],
        out_specs=pl.BlockSpec(memory_space=pltpu.VMEM),
        scratch_shapes=[
            pltpu.VMEM((windows, chl, length), bf),
            pltpu.VMEM((length, 2 * NBINS), bf),
            pltpu.VMEM((windows * BLOCK, 2 * NBINS), f32),
            pltpu.VMEM((GROUPS, chl, 128), bf),
            pltpu.VMEM((sub, chans * nch, BLOCK, 128), bf),
            pltpu.VMEM((sub, chans * nch, BLOCK, 128), bf),
            pltpu.VMEM((planes, spp, 2 * BLOCK, BLOCK), bf),
            pltpu.VMEM((planes, spp, 2 * BLOCK, BLOCK), bf),
            pltpu.VMEM((spp, 2 * BLOCK, BLOCK), bf),
            pltpu.VMEM((sub, spd, 2 * BLOCK, BLOCK), f32),
            pltpu.VMEM((spp, 2 * BLOCK, BLOCK), f32),
            pltpu.SemaphoreType.DMA(((nch + 1) * KCH,)),
            pltpu.SemaphoreType.DMA((nch,)),
            pltpu.SemaphoreType.DMA((nch, GROUPS)),
            pltpu.SemaphoreType.DMA((nch, GROUPS)),
            pltpu.SemaphoreType.DMA((planes, spp)),
            pltpu.SemaphoreType.DMA((planes, spp)),
            pltpu.SemaphoreType.DMA((spp,)),
            pltpu.SemaphoreType.DMA((spp,)),
            pltpu.SemaphoreType.DMA((sub, spd)),
        ],
        compiler_params=pltpu.CompilerParams(
            collective_id=0, has_side_effects=True, vmem_limit_bytes=60 * 1024 * 1024
        ),
        cost_estimate=pl.CostEstimate(
            flops=2 * windows * chl * length * 2 * NBINS,
            bytes_accessed=2 * (windows * chl * length + length * 2 * NBINS),
            transcendentals=0,
        ),
    )(traces, table, block_pairs)
    stack_scale = 1.0 / math.sqrt(windows * planes * sub * GROUP)
    slot_ids = lax.axis_index("win") * spd + jnp.arange(spd, dtype=jnp.int32)
    live = (slot_ids < valid_count[0]).astype(f32)
    sums = sums.reshape(spd, sub, 2, BLOCK, BLOCK)
    return sums * (stack_scale * live)[:, None, None, None, None]


def solution(mesh):
    wins, chans = mesh.shape["win"], mesh.shape["chan"]
    sub = GROUPS // chans
    planes = wins // sub

    def run(traces, block_pairs, valid_count):
        table = jnp.asarray(dft_table(traces.shape[2]))
        body = functools.partial(on_device, planes, sub, chans)
        return jax.shard_map(
            body,
            mesh=mesh,
            in_specs=(P(), P("win", "chan", None), P(), P()),
            out_specs=P("win", "chan", None, None, None),
            check_vma=False,
        )(table, traces, block_pairs, valid_count)

    return run
```

time: 196 us -> 46.2 us (0.24)
  the two profiles are of different devices: /device:TPU:8 before, /device:TPU:1 now
where the time goes in v1:
time: 46.2 us; the launch traced here: 46 us
  Pallas kernels  42.1 us (91%)
  other arithmetic  1.87 us (4%)
  local copies, waits for them, and re-layouts  1.35 us (3%)
  between operations  0.66 us (1%)
    pallas_call x1, Pallas kernels, on_device(): pl.pallas_call(functools.partial(kernel, dims), name='cross_spectra', out...  42.1 us
    mul x1, other arithmetic, on_device(): return sums * (stack_scale * live)[:, None, None, None, None]  1.87 us
    unnamed x1, local copies, waits for them, and re-layouts  1.35 us

profile of v1, /device:TPU:1, one launch (start us, length us, event | category | flops | bytes accessed | tf_op | source)
XLA Modules:
  0.0 46.0 jit_solution(5473469408885962564)
XLA Ops:
  0.0 1.4 %copy.5.pairs = s32[16,2]{1,0:T(8,128)} copy(s32[16,2]{0,1:T(2,128)} %param.5) | data formatting | bytes 256 | tf_op args[1]
  1.4 42.1 %cross_spectra.1 = f32[1,4,256,128]{3,2,1,0:T(8,128)} custom-call(bf16[2,256,4096]{2,1,0:T(8,128)(2,1)} %tr_hbm.1, bf16[4096,512]{1,0:T(8,128)(2,1)} %constant.13.clone.table_hbm, s32[16,2]{1,0:T(8,128)} %copy.5.pairs), custom_call_target="tpu_custom_call" | custom-call | flops 2147483648 | bytes 8388608 | tf_op jit(solution)/shard_map/cross_spectra/pallas_call | solution.py:340
  44.1 1.9 %broadcast_multiply_fusion = f32[1,4,256,128]{3,2,1,0:T(8,128)} fusion(f32[1,4,256,128]{3,2,1,0:T(8,128)} %cross_spectra.1, f32[]{:T(128)} %bitcast.1), kind=kLoop, calls=%fused_computation | loop fusion | flops 131072 | bytes 1048580 | tf_op jit(solution)/shard_map/mul | solution.py:385

commit v2 on v1

v2 whole, which is shorter than its diff:
```python
import functools
import math

import jax
import jax.numpy as jnp
import ml_dtypes
import numpy as np
from jax import lax
from jax.experimental import pallas as pl
from jax.experimental.pallas import tpu as pltpu
from jax.sharding import PartitionSpec as P

BLOCK = 128
NBINS = 256
FREQ_LO = 64
GROUP = 32
GROUPS = NBINS // GROUP
EPS = 1e-06
MESH = pl.DeviceIdType.MESH
KCH = 4


def dft_table(length):
    times = np.arange(length, dtype=np.int32)
    freqs = FREQ_LO + np.arange(NBINS, dtype=np.int32)
    phases = times[:, None] * freqs[None, :] % length
    angles = phases.astype(np.float32) * np.float32(2.0 * math.pi / length)
    wide = angles.astype(np.float64)
    factor = np.float32(1.0 / math.sqrt(length))
    re = np.cos(wide).astype(np.float32) * factor
    im = -np.sin(wide).astype(np.float32) * factor
    table = np.stack(
        [re.reshape(length, GROUPS, GROUP), im.reshape(length, GROUPS, GROUP)], axis=2
    )
    return table.reshape(length, 2 * NBINS).astype(ml_dtypes.bfloat16)


def kernel(
    dims, tr_hbm, table_hbm, pairs, out,
    tr, table, acc, send, held, turned, held2, turned2, outbox, inbox, relay, value,
    in_sem, self_sem, a_send, a_recv, h_send, h_recv, p_send, p_recv, r_recv,
):
    planes, sub, chans, spp, spd, chl, length, relayed, forwards = dims
    win, x = lax.axis_index("win"), lax.axis_index("chan")
    q, j = win // sub, win % sub
    g = x * sub + j
    kc = length // KCH
    nch = chl // BLOCK
    both = jnp.logical_and
    last = planes - 1
    end = jnp.logical_or(q == 0, q == last)
    inner = jnp.logical_or(q == 1, q == last - 1)
    partner = jnp.where(q == 0, 1, jnp.where(q == 1, 0, jnp.where(q == last, last - 1, last)))
    by_data = (j % 2 == 0) if forwards else (j < 0)

    def tr_copy(c, k):
        part = (slice(None), pl.ds(c * BLOCK, BLOCK), pl.ds(k * kc, kc))
        return pltpu.make_async_copy(tr_hbm.at[part], tr.at[part], in_sem.at[c * KCH + k])

    def table_copy(k):
        part = pl.ds(k * kc, kc)
        return pltpu.make_async_copy(table_hbm.at[part], table.at[part], in_sem.at[nch * KCH + k])

    for k in range(KCH):
        tr_copy(0, k).start()
        table_copy(k).start()
    for c in range(1, nch):
        for k in range(KCH):
            tr_copy(c, k).start()

    barrier = pltpu.get_barrier_semaphore()

    @pl.loop(sub, GROUPS)
    def _(o):
        to = ((x * sub) + o) % GROUPS
        pl.semaphore_signal(
            barrier, inc=1, device_id=(q * sub + to % sub, to // sub), device_id_type=MESH
        )

    @pl.loop(1, planes * sub)
    def _(o):
        pl.semaphore_signal(
            barrier, inc=1, device_id=((win + o) % (planes * sub), x), device_id_type=MESH
        )

    def a_copy(c, o, to):
        return pltpu.make_async_remote_copy(
            src_ref=send.at[to, pl.ds(c * BLOCK, BLOCK), :],
            dst_ref=held.at[j, x * nch + c],
            send_sem=a_send.at[c, o],
            recv_sem=a_recv.at[c, o],
            device_id=(q * sub + to % sub, to // sub),
            device_id_type=MESH,
        )

    def h_copy(c, src):
        b = (src // sub) * nch + c
        return pltpu.make_async_remote_copy(
            src_ref=held.at[src % sub, b],
            dst_ref=held2.at[src % sub, b],
            send_sem=h_send.at[c, src],
            recv_sem=h_recv.at[c, src],
            device_id=(partner * sub + j, x),
            device_id_type=MESH,
        )

    def forward(c, src):
        if forwards:

            @pl.when(both(end, by_data))
            def _():
                h_copy(c, src).start()

    low = lax.broadcasted_iota(jnp.int32, (BLOCK, 128), 1) < 2 * GROUP
    for c in range(nch):
        for k in range(KCH):
            tr_copy(c, k).wait()
            if c == 0:
                table_copy(k).wait()
            rows = tr[:, c * BLOCK : (c + 1) * BLOCK, k * kc : (k + 1) * kc]
            term = jnp.dot(
                rows.reshape(2 * BLOCK, kc),
                table[k * kc : (k + 1) * kc, :],
                preferred_element_type=jnp.float32,
            )
            if k == 0:
                acc[...] = term
            else:
                acc[...] += term
        spectra = acc[...]
        energy = jnp.sum(spectra * spectra, axis=1, keepdims=True) / NBINS
        white = spectra * lax.rsqrt(energy + EPS)
        for h in range(GROUPS // 2):
            a = white[:BLOCK, h * 128 : (h + 1) * 128]
            b = white[BLOCK:, h * 128 : (h + 1) * 128]
            even = jnp.where(low, a, pltpu.roll(b, 64, 1))
            odd = jnp.where(low, pltpu.roll(a, 64, 1), b)
            send[2 * h, c * BLOCK : (c + 1) * BLOCK, :] = even.astype(jnp.bfloat16)
            send[2 * h + 1, c * BLOCK : (c + 1) * BLOCK, :] = odd.astype(jnp.bfloat16)
        if c == 0:
            pl.semaphore_wait(barrier, GROUPS - sub + planes * sub - 1)

        @pl.loop(1, GROUPS)
        def _(o):
            a_copy(c, o, (g + o) % GROUPS).start()

        pltpu.make_async_copy(
            send.at[g, pl.ds(c * BLOCK, BLOCK), :],
            held.at[j, x * nch + c],
            self_sem.at[c],
        ).start()

    for c in range(nch):
        pltpu.make_async_copy(
            send.at[g, pl.ds(c * BLOCK, BLOCK), :],
            held.at[j, x * nch + c],
            self_sem.at[c],
        ).wait()
        forward(c, g)

        @pl.loop(1, GROUPS)
        def _(o):
            src = (g + GROUPS - o) % GROUPS
            pltpu.make_async_remote_copy(
                src_ref=send.at[src, pl.ds(c * BLOCK, BLOCK), :],
                dst_ref=held.at[src % sub, (src // sub) * nch + c],
                send_sem=a_send.at[c, o],
                recv_sem=a_recv.at[c, o],
                device_id=(q * sub + src % sub, src // sub),
                device_id_type=MESH,
            ).wait_recv()
            forward(c, src)

    row = lax.broadcasted_iota(jnp.int32, (128, 128), 0)
    col = lax.broadcasted_iota(jnp.int32, (128, 128), 1)
    turn = jnp.where(
        col % (2 * GROUP) < GROUP,
        jnp.where(row == col + GROUP, 1.0, 0.0),
        jnp.where(row + GROUP == col, -1.0, 0.0),
    ).astype(jnp.bfloat16)

    def turn_all(held, turned):
        @pl.loop(0, chans * nch)
        def _(b):
            for m in range(sub):
                turned[m, b] = jnp.dot(
                    held[m, b], turn, preferred_element_type=jnp.float32
                ).astype(jnp.bfloat16)

    turn_all(held, turned)

    def partial(p, held, turned):
        r, s = pairs[0, p], pairs[1, p]
        ms = range(sub)
        upper = jnp.concatenate(
            [
                jnp.concatenate([held[m, r] for m in ms], axis=1),
                jnp.concatenate([turned[m, r] for m in ms], axis=1),
            ],
            axis=0,
        )
        lower = jnp.concatenate([held[m, s] for m in ms], axis=1)
        return lax.dot_general(
            upper, lower, (((1,), (1,)), ((), ())), preferred_element_type=jnp.float32
        )

    def dest(k):
        return jnp.where(q < planes // 2, (q + planes - k) % planes, (q + k) % planes)

    def p_copy(d, i, t):
        return pltpu.make_async_remote_copy(
            src_ref=outbox.at[d, i],
            dst_ref=inbox.at[q, j, t % spd],
            send_sem=p_send.at[d, i],
            recv_sem=p_recv.at[q, j, t % spd],
            device_id=(d * sub + t // spd, x),
            device_id_type=MESH,
        )

    def r_copy(d, i):
        return pltpu.make_async_remote_copy(
            src_ref=outbox.at[d, i],
            dst_ref=relay.at[d, i],
            send_sem=p_send.at[d, i],
            recv_sem=r_recv.at[d, i],
            device_id=(partner * sub + j, x),
            device_id_type=MESH,
        )

    def item(n):
        d, i = dest(n // spp + 1), n % spp
        t = (j * spd + spd + i) % spp
        local = both(d == q, t // spd == j)
        return d, i, t, local

    @pl.loop(0, planes * spp)
    def _(n):
        d, i, t, local = item(n)
        if forwards:

            @pl.when(both(inner, both(by_data, n == spp)))
            def _():
                for c in range(nch):

                    @pl.loop(0, GROUPS)
                    def _(src):
                        h_copy(c, src).wait_recv()

                turn_all(held2, turned2)

        def work():
            value[...] = partial(d * spp + t, held, turned)
            if forwards:

                @pl.when(both(inner, both(by_data, d != partner)))
                def _():
                    value[...] += partial(d * spp + t, held2, turned2)

            if relayed:

                @pl.when(both(both(inner, jnp.logical_not(by_data)), both(d != partner, d != q)))
                def _():
                    r_copy(d, i).wait_recv()
                    value[...] += relay[d, i].astype(jnp.float32)

            @pl.when(local)
            def _():
                out[t % spd, j] = value[...]

            @pl.when(jnp.logical_not(local))
            def _():
                outbox[d, i] = value[...].astype(jnp.bfloat16)
                if relayed:
                    via = both(end, both(d != q, d != partner))

                    @pl.when(via)
                    def _():
                        r_copy(d, i).start()

                    @pl.when(jnp.logical_not(via))
                    def _():
                        p_copy(d, i, t).start()

                else:
                    p_copy(d, i, t).start()

        if forwards:
            pl.when(jnp.logical_not(both(both(end, by_data), d != q)))(work)
        else:
            work()

    def exists(src, m):
        there = jnp.logical_not(both(src == q, m == j))
        if relayed:
            src_end = jnp.logical_or(src == 0, src == last)
            src_partner = jnp.where(src == 0, 1, last - 1)
            direct = src_partner == q
            if forwards:
                direct = both(direct, m % 2 == 1)
            there = both(
                there, jnp.logical_or(src == q, jnp.logical_or(jnp.logical_not(src_end), direct))
            )
        return there

    @pl.loop(0, planes * sub)
    def _(n):
        src, m = (q + n // sub) % planes, n % sub

        @pl.when(exists(src, m))
        def _():
            for e in range(spd):
                pltpu.make_async_remote_copy(
                    src_ref=outbox.at[0, 0],
                    dst_ref=inbox.at[src, m, e],
                    send_sem=p_send.at[0, 0],
                    recv_sem=p_recv.at[src, m, e],
                    device_id=(src * sub + m, x),
                    device_id_type=MESH,
                ).wait_recv()
                got = inbox[src, m, e].astype(jnp.float32)

                @pl.when(both(n < sub, m != j))
                def _():
                    out[e, m] = got

                @pl.when(jnp.logical_not(both(n < sub, m != j)))
                def _():
                    out[e, m] += got

    for c in range(nch):

        @pl.loop(1, GROUPS)
        def _(o):
            a_copy(c, o, (g + o) % GROUPS).wait_send()

        if forwards:

            @pl.when(both(end, by_data))
            def _():
                @pl.loop(0, GROUPS)
                def _(src):
                    h_copy(c, src).wait_send()

    @pl.loop(0, planes * spp)
    def _(n):
        d, i, t, local = item(n)
        sent = jnp.logical_not(local)
        if forwards:
            sent = both(sent, jnp.logical_not(both(both(end, by_data), d != q)))

        @pl.when(sent)
        def _():
            p_copy(d, i, t).wait_send()


def on_device(planes, sub, chans, table, traces, block_pairs, valid_count):
    windows, chl, length = traces.shape
    slots = block_pairs.shape[0]
    spp, spd = slots // planes, slots // (planes * sub)
    relayed = planes >= 4
    dims = (planes, sub, chans, spp, spd, chl, length, relayed, relayed and sub > 1)
    bf, f32 = jnp.bfloat16, jnp.float32
    nch = chl // BLOCK
    sums = pl.pallas_call(
        functools.partial(kernel, dims),
        name="cross_spectra",
        out_shape=jax.ShapeDtypeStruct((spd, sub, 2 * BLOCK, BLOCK), f32),
        in_specs=[
            pl.BlockSpec(memory_space=pl.ANY),
            pl.BlockSpec(memory_space=pl.ANY),
            pl.BlockSpec(memory_space=pltpu.SMEM),
        ],
        out_specs=pl.BlockSpec(memory_space=pltpu.VMEM),
        scratch_shapes=[
            pltpu.VMEM((windows, chl, length), bf),
            pltpu.VMEM((length, 2 * NBINS), bf),
            pltpu.VMEM((windows * BLOCK, 2 * NBINS), f32),
            pltpu.VMEM((GROUPS, chl, 128), bf),
            pltpu.VMEM((sub, chans * nch, BLOCK, 128), bf),
            pltpu.VMEM((sub, chans * nch, BLOCK, 128), bf),
            pltpu.VMEM((sub, chans * nch, BLOCK, 128), bf),
            pltpu.VMEM((sub, chans * nch, BLOCK, 128), bf),
            pltpu.VMEM((planes, spp, 2 * BLOCK, BLOCK), bf),
            pltpu.VMEM((planes, sub, spd, 2 * BLOCK, BLOCK), bf),
            pltpu.VMEM((planes, spp, 2 * BLOCK, BLOCK), bf),
            pltpu.VMEM((2 * BLOCK, BLOCK), f32),
            pltpu.SemaphoreType.DMA(((nch + 1) * KCH,)),
            pltpu.SemaphoreType.DMA((nch,)),
            pltpu.SemaphoreType.DMA((nch, GROUPS)),
            pltpu.SemaphoreType.DMA((nch, GROUPS)),
            pltpu.SemaphoreType.DMA((nch, GROUPS)),
            pltpu.SemaphoreType.DMA((nch, GROUPS)),
            pltpu.SemaphoreType.DMA((planes, spp)),
            pltpu.SemaphoreType.DMA((planes, sub, spd)),
            pltpu.SemaphoreType.DMA((planes, spp)),
        ],
        compiler_params=pltpu.CompilerParams(
            collective_id=0, has_side_effects=True, vmem_limit_bytes=60 * 1024 * 1024
        ),
        cost_estimate=pl.CostEstimate(
            flops=2 * windows * chl * length * 2 * NBINS,
            bytes_accessed=2 * (windows * chl * length + length * 2 * NBINS),
            transcendentals=0,
        ),
    )(traces, table, block_pairs.T)
    stack_scale = 1.0 / math.sqrt(windows * planes * sub * GROUP)
    slot_ids = lax.axis_index("win") * spd + jnp.arange(spd, dtype=jnp.int32)
    live = (slot_ids < valid_count[0]).astype(f32)
    sums = sums.reshape(spd, sub, 2, BLOCK, BLOCK)
    return sums * (stack_scale * live)[:, None, None, None, None]


def solution(mesh):
    wins, chans = mesh.shape["win"], mesh.shape["chan"]
    sub = GROUPS // chans
    planes = wins // sub

    def run(traces, block_pairs, valid_count):
        table = jnp.asarray(dft_table(traces.shape[2]))
        body = functools.partial(on_device, planes, sub, chans)
        return jax.shard_map(
            body,
            mesh=mesh,
            in_specs=(P(), P("win", "chan", None), P(), P()),
            out_specs=P("win", "chan", None, None, None),
            check_vma=False,
        )(table, traces, block_pairs, valid_count)

    return run
```

time: 46.2 us -> 36.9 us (0.80)
  the two profiles are of different devices: /device:TPU:1 before, /device:TPU:8 now
where the time goes in v2:
time: 36.9 us; the launch traced here: 36.7 us
  Pallas kernels  34.2 us (93%)
  other arithmetic  1.87 us (5%)
  between operations  0.66 us (2%)
    pallas_call x1, Pallas kernels, on_device(): pl.pallas_call(functools.partial(kernel, dims), name='cross_spectra', out...  34.2 us
    mul x1, other arithmetic, on_device(): return sums * (stack_scale * live)[:, None, None, None, None]  1.87 us

profile of v2, /device:TPU:8, one launch (start us, length us, event | category | flops | bytes accessed | tf_op | source)
XLA Modules:
  0.0 36.7 jit_solution(8718279706123070846)
XLA Ops:
  0.7 34.2 %cross_spectra.1 = f32[1,4,256,128]{3,2,1,0:T(8,128)} custom-call(bf16[2,256,4096]{2,1,0:T(8,128)(2,1)} %tr_hbm.1, bf16[4096,512]{1,0:T(8,128)(2,1)} %constant.13.clone.table_hbm, s32[2,16]{1,0:T(2,128)} %bitcast.4), custom_call_target="tpu_custom_call" | custom-call | flops 2147483648 | bytes 8388608 | tf_op jit(solution)/shard_map/cross_spectra/pallas_call | solution.py:364
  34.8 1.9 %broadcast_multiply_fusion = f32[1,4,256,128]{3,2,1,0:T(8,128)} fusion(f32[1,4,256,128]{3,2,1,0:T(8,128)} %cross_spectra.1, f32[]{:T(128)} %bitcast.2), kind=kLoop, calls=%fused_computation | loop fusion | flops 131072 | bytes 1048580 | tf_op jit(solution)/shard_map/mul | solution.py:410

commit v3 on v2

--- a/solution.py
+++ b/solution.py
@@ -189,17 +189,16 @@
 
     turn_all(held, turned)
 
-    def partial(p, held, turned):
+    def partial(p, parts):
         r, s = pairs[0, p], pairs[1, p]
-        ms = range(sub)
         upper = jnp.concatenate(
             [
-                jnp.concatenate([held[m, r] for m in ms], axis=1),
-                jnp.concatenate([turned[m, r] for m in ms], axis=1),
+                jnp.concatenate([have[m, r] for have, _ in parts for m in range(sub)], axis=1),
+                jnp.concatenate([turn[m, r] for _, turn in parts for m in range(sub)], axis=1),
             ],
             axis=0,
         )
-        lower = jnp.concatenate([held[m, s] for m in ms], axis=1)
+        lower = jnp.concatenate([have[m, s] for have, _ in parts for m in range(sub)], axis=1)
         return lax.dot_general(
             upper, lower, (((1,), (1,)), ((), ())), preferred_element_type=jnp.float32
         )
@@ -228,7 +227,10 @@
         )
 
     def item(n):
-        d, i = dest(n // spp + 1), n % spp
+        k = n // spp
+        if forwards:
+            k = jnp.where(both(both(inner, by_data), k < last), (k + 1) % last, k)
+        d, i = dest(k + 1), n % spp
         t = (j * spd + spd + i) % spp
         local = both(d == q, t // spd == j)
         return d, i, t, local
@@ -238,7 +240,7 @@
         d, i, t, local = item(n)
         if forwards:
 
-            @pl.when(both(inner, both(by_data, n == spp)))
+            @pl.when(both(inner, both(by_data, n == 0)))
             def _():
                 for c in range(nch):
 
@@ -249,12 +251,20 @@
                 turn_all(held2, turned2)
 
         def work():
-            value[...] = partial(d * spp + t, held, turned)
+            own = [(held, turned)]
             if forwards:
-
-                @pl.when(both(inner, both(by_data, d != partner)))
+                wide = both(inner, both(by_data, d != partner))
+
+                @pl.when(wide)
                 def _():
-                    value[...] += partial(d * spp + t, held2, turned2)
+                    value[...] = partial(d * spp + t, own + [(held2, turned2)])
+
+                @pl.when(jnp.logical_not(wide))
+                def _():
+                    value[...] = partial(d * spp + t, own)
+
+            else:
+                value[...] = partial(d * spp + t, own)
 
             if relayed:
 
@@ -395,7 +405,7 @@
             pltpu.SemaphoreType.DMA((planes, spp)),
         ],
         compiler_params=pltpu.CompilerParams(
-            collective_id=0, has_side_effects=True, vmem_limit_bytes=60 * 1024 * 1024
+            collective_id=0, has_side_effects=True, vmem_limit_bytes=51 * 1024 * 1024
         ),
         cost_estimate=pl.CostEstimate(
             flops=2 * windows * chl * length * 2 * NBINS,

time: 36.9 us -> 35.7 us (0.967)
  other arithmetic: 1.87 us -> 0.83 us
  Pallas kernels: 34.2 us -> 33.3 us
  local copies, waits for them, and re-layouts: 0 us -> 0.67 us
    mul x1, other arithmetic: 1.87 us -> 0.83 us  [on_device(): return sums * (stack_scale * live)[:, None, None, None, None]]
    pallas_call x1, Pallas kernels: 34.2 us -> 33.3 us  [on_device(): pl.pallas_call(functools.partial(kernel, dims), name='cross_spectra', out...]
    unnamed x0 -> x2, local copies, waits for them, and re-layouts: none -> 0.67 us
where the time goes in v3:
time: 35.7 us; the launch traced here: 35.5 us
  Pallas kernels  33.3 us (93%)
  other arithmetic  0.83 us (2%)
  local copies, waits for them, and re-layouts  0.67 us (2%)
  between operations  0.67 us (2%)
    pallas_call x1, Pallas kernels, on_device(): pl.pallas_call(functools.partial(kernel, dims), name='cross_spectra', out...  33.3 us
    mul x1, other arithmetic, on_device(): return sums * (stack_scale * live)[:, None, None, None, None]  0.83 us

profile of v3, /device:TPU:8, one launch (start us, length us, event | category | flops | bytes accessed | tf_op | source)
XLA Modules:
  0.0 35.5 jit_solution(6683631427166744744)
XLA Ops:
  0.7 0.0 copy-start
  0.7 0.7 %copy-done = s32[16,2]{0,1:T(2,128)S(1)} copy-done((s32[16,2]{0,1:T(2,128)S(1)}, s32[16,2]{0,1:T(2,128)}, u32[]{:S(2)}) %copy-start) | copy-done | bytes 152
  1.3 33.3 %cross_spectra.1 = f32[1,4,256,128]{3,2,1,0:T(8,128)S(1)} custom-call(bf16[2,256,4096]{2,1,0:T(8,128)(2,1)} %tr_hbm.1, bf16[4096,512]{1,0:T(8,128)(2,1)} %constant.13.clone.table_hbm, s32[2,16]{1,0:T(2,128)S(1)} %bitcast.4), custom_call_target="tpu_custom_call" | custom-call | flops 2147483648 | bytes 8388608 | tf_op jit(solution)/shard_map/cross_spectra/pallas_call | solution.py:374
  34.7 0.8 %broadcast_multiply_fusion = f32[1,4,256,128]{3,2,1,0:T(8,128)} fusion(f32[1,4,256,128]{3,2,1,0:T(8,128)S(1)} %cross_spectra.1, f32[]{:T(128)} %bitcast.2), kind=kLoop, calls=%fused_computation | loop fusion | flops 131072 | bytes 1048580 | tf_op jit(solution)/shard_map/mul | solution.py:420
Async XLA Ops:
  0.7 0.7 %copy-start = (s32[16,2]{0,1:T(2,128)S(1)}, s32[16,2]{0,1:T(2,128)}, u32[]{:S(2)}) copy-start(s32[16,2]{0,1:T(2,128)} %param.5) | copy-start | bytes 388

commit v4 on v3

--- a/solution.py
+++ b/solution.py
@@ -36,9 +36,9 @@
 
 
 def kernel(
-    dims, tr_hbm, table_hbm, pairs, out,
-    tr, table, acc, send, held, turned, held2, turned2, outbox, inbox, relay, value,
-    in_sem, self_sem, a_send, a_recv, h_send, h_recv, p_send, p_recv, r_recv,
+    dims, tr_hbm, table_hbm, pairs_hbm, out,
+    tr, table, acc, send, held, turned, flipped, held2, turned2, flipped2, outbox, inbox, relay, value, pairs,
+    in_sem, pairs_sem, self_sem, a_send, a_recv, h_send, h_recv, p_send, p_recv, r_recv,
 ):
     planes, sub, chans, spp, spd, chl, length, relayed, forwards = dims
     win, x = lax.axis_index("win"), lax.axis_index("chan")
@@ -68,6 +68,9 @@
         for k in range(KCH):
             tr_copy(c, k).start()
 
+    pairs_copy = pltpu.make_async_copy(pairs_hbm, pairs, pairs_sem)
+    pairs_copy.start()
+
     barrier = pltpu.get_barrier_semaphore()
 
     @pl.loop(sub, GROUPS)
@@ -110,6 +113,25 @@
             @pl.when(both(end, by_data))
             def _():
                 h_copy(c, src).start()
+
+    row = lax.broadcasted_iota(jnp.int32, (128, 128), 0)
+    col = lax.broadcasted_iota(jnp.int32, (128, 128), 1)
+    turn = jnp.where(
+        col % (2 * GROUP) < GROUP,
+        jnp.where(row == col + GROUP, 1.0, 0.0),
+        jnp.where(row + GROUP == col, -1.0, 0.0),
+    ).astype(jnp.bfloat16)
+    eye = jnp.where(row == col, 1.0, 0.0).astype(jnp.bfloat16)
+
+    def prepare(c, src, held, turned, flipped):
+        m, b = src % sub, (src // sub) * nch + c
+        piece = held[m, b]
+        turned[m, b] = jnp.dot(piece, turn, preferred_element_type=jnp.float32).astype(
+            jnp.bfloat16
+        )
+        flipped[m, b] = lax.dot_general(
+            eye, piece, (((1,), (1,)), ((), ())), preferred_element_type=jnp.float32
+        ).astype(jnp.bfloat16)
 
     low = lax.broadcasted_iota(jnp.int32, (BLOCK, 128), 1) < 2 * GROUP
     for c in range(nch):
@@ -157,6 +179,7 @@
             self_sem.at[c],
         ).wait()
         forward(c, g)
+        prepare(c, g, held, turned, flipped)
 
         @pl.loop(1, GROUPS)
         def _(o):
@@ -170,38 +193,19 @@
                 device_id_type=MESH,
             ).wait_recv()
             forward(c, src)
-
-    row = lax.broadcasted_iota(jnp.int32, (128, 128), 0)
-    col = lax.broadcasted_iota(jnp.int32, (128, 128), 1)
-    turn = jnp.where(
-        col % (2 * GROUP) < GROUP,
-        jnp.where(row == col + GROUP, 1.0, 0.0),
-        jnp.where(row + GROUP == col, -1.0, 0.0),
-    ).astype(jnp.bfloat16)
-
-    def turn_all(held, turned):
-        @pl.loop(0, chans * nch)
-        def _(b):
-            for m in range(sub):
-                turned[m, b] = jnp.dot(
-                    held[m, b], turn, preferred_element_type=jnp.float32
-                ).astype(jnp.bfloat16)
-
-    turn_all(held, turned)
+            prepare(c, src, held, turned, flipped)
 
     def partial(p, parts):
         r, s = pairs[0, p], pairs[1, p]
         upper = jnp.concatenate(
             [
-                jnp.concatenate([have[m, r] for have, _ in parts for m in range(sub)], axis=1),
-                jnp.concatenate([turn[m, r] for _, turn in parts for m in range(sub)], axis=1),
+                jnp.concatenate([have[m, r] for have, _, _ in parts for m in range(sub)], axis=1),
+                jnp.concatenate([rot[m, r] for _, rot, _ in parts for m in range(sub)], axis=1),
             ],
             axis=0,
         )
-        lower = jnp.concatenate([have[m, s] for have, _ in parts for m in range(sub)], axis=1)
-        return lax.dot_general(
-            upper, lower, (((1,), (1,)), ((), ())), preferred_element_type=jnp.float32
-        )
+        lower = jnp.concatenate([flip[m, s] for _, _, flip in parts for m in range(sub)], axis=0)
+        return jnp.dot(upper, lower, preferred_element_type=jnp.float32)
 
     def dest(k):
         return jnp.where(q < planes // 2, (q + planes - k) % planes, (q + k) % planes)
@@ -235,6 +239,8 @@
         local = both(d == q, t // spd == j)
         return d, i, t, local
 
+    pairs_copy.wait()
+
     @pl.loop(0, planes * spp)
     def _(n):
         d, i, t, local = item(n)
@@ -247,17 +253,17 @@
                     @pl.loop(0, GROUPS)
                     def _(src):
                         h_copy(c, src).wait_recv()
-
-                turn_all(held2, turned2)
+                        prepare(c, src, held2, turned2, flipped2)
+
 
         def work():
-            own = [(held, turned)]
+            own = [(held, turned, flipped)]
             if forwards:
                 wide = both(inner, both(by_data, d != partner))
 
                 @pl.when(wide)
                 def _():
-                    value[...] = partial(d * spp + t, own + [(held2, turned2)])
+                    value[...] = partial(d * spp + t, own + [(held2, turned2, flipped2)])
 
                 @pl.when(jnp.logical_not(wide))
                 def _():
@@ -376,9 +382,9 @@
         name="cross_spectra",
         out_shape=jax.ShapeDtypeStruct((spd, sub, 2 * BLOCK, BLOCK), f32),
         in_specs=[
-            pl.BlockSpec(memory_space=pl.ANY),
-            pl.BlockSpec(memory_space=pl.ANY),
-            pl.BlockSpec(memory_space=pltpu.SMEM),
+            pl.BlockSpec(memory_space=pltpu.HBM),
+            pl.BlockSpec(memory_space=pltpu.HBM),
+            pl.BlockSpec(memory_space=pltpu.HBM),
         ],
         out_specs=pl.BlockSpec(memory_space=pltpu.VMEM),
         scratch_shapes=[
@@ -390,11 +396,15 @@
             pltpu.VMEM((sub, chans * nch, BLOCK, 128), bf),
             pltpu.VMEM((sub, chans * nch, BLOCK, 128), bf),
             pltpu.VMEM((sub, chans * nch, BLOCK, 128), bf),
+            pltpu.VMEM((sub, chans * nch, BLOCK, 128), bf),
+            pltpu.VMEM((sub, chans * nch, BLOCK, 128), bf),
             pltpu.VMEM((planes, spp, 2 * BLOCK, BLOCK), bf),
             pltpu.VMEM((planes, sub, spd, 2 * BLOCK, BLOCK), bf),
             pltpu.VMEM((planes, spp, 2 * BLOCK, BLOCK), bf),
             pltpu.VMEM((2 * BLOCK, BLOCK), f32),
+            pltpu.SMEM((2, slots), jnp.int32),
             pltpu.SemaphoreType.DMA(((nch + 1) * KCH,)),
+            pltpu.SemaphoreType.DMA,
             pltpu.SemaphoreType.DMA((nch,)),
             pltpu.SemaphoreType.DMA((nch, GROUPS)),
             pltpu.SemaphoreType.DMA((nch, GROUPS)),

time: 35.7 us -> 35.1 us (0.983)
  Pallas kernels: 33.3 us -> 32.7 us
    pallas_call x1, Pallas kernels: 33.3 us -> 32.7 us  [on_device(): pl.pallas_call(functools.partial(kernel, dims), name='cross_spectra', out...]
where the time goes in v4:
time: 35.1 us; the launch traced here: 34.9 us
  Pallas kernels  32.7 us (93%)
  other arithmetic  0.83 us (2%)
  local copies, waits for them, and re-layouts  0.67 us (2%)
  between operations  0.67 us (2%)
    pallas_call x1, Pallas kernels, on_device(): pl.pallas_call(functools.partial(kernel, dims), name='cross_spectra', out...  32.7 us
    mul x1, other arithmetic, on_device(): return sums * (stack_scale * live)[:, None, None, None, None]  0.83 us

profile of v4, /device:TPU:8, one launch (start us, length us, event | category | flops | bytes accessed | tf_op | source)
XLA Modules:
  0.0 34.9 jit_solution(2104606329390535714)
XLA Ops:
  0.7 0.0 copy-start
  0.7 0.7 %copy-done = s32[16,2]{0,1:T(2,128)S(1)} copy-done((s32[16,2]{0,1:T(2,128)S(1)}, s32[16,2]{0,1:T(2,128)}, u32[]{:S(2)}) %copy-start) | copy-done | bytes 152
  1.3 32.7 %cross_spectra.1 = f32[1,4,256,128]{3,2,1,0:T(8,128)S(1)} custom-call(bf16[2,256,4096]{2,1,0:T(8,128)(2,1)} %tr_hbm.1, bf16[4096,512]{1,0:T(8,128)(2,1)} %constant.13.clone.table_hbm, s32[2,16]{1,0:T(2,128)S(1)} %bitcast.4), custom_call_target="tpu_custom_call" | custom-call | flops 2147483648 | bytes 8388608 | tf_op jit(solution)/shard_map/cross_spectra/pallas_call | solution.py:380
  34.0 0.8 %broadcast_multiply_fusion = f32[1,4,256,128]{3,2,1,0:T(8,128)} fusion(f32[1,4,256,128]{3,2,1,0:T(8,128)S(1)} %cross_spectra.1, f32[]{:T(128)} %bitcast.2), kind=kLoop, calls=%fused_computation | loop fusion | flops 131072 | bytes 1048580 | tf_op jit(solution)/shard_map/mul | solution.py:430
Async XLA Ops:
  0.7 0.7 %copy-start = (s32[16,2]{0,1:T(2,128)S(1)}, s32[16,2]{0,1:T(2,128)}, u32[]{:S(2)}) copy-start(s32[16,2]{0,1:T(2,128)} %param.5) | copy-start | bytes 388
